TPU v7x, 128 devices: a whole 4x4x4 slice. The times are simulated.
128 devices in a mesh: dp: 32 (over x_hi, y, z), tensor: 4 (over x_lo, core).
Axes of the slice: x: 4 (x_hi: 2, x_lo: 2; x = x_hi * 2 + x_lo), y: 4, z: 4, core: 2. Of those that a mesh axis runs over, the one named last changes fastest.
Arguments:
- inputs: bfloat16 [32768, 640], P('dp'), may hold values from -6 to 6
- segments: int32 [32768], P('dp'), may hold values from 0 to 63, never falling along the last dimension, each value on 1 to 2048 neighbouring positions
- positions: int32 [32768], P('dp'), may hold values from 0 to 2047
- cotangent: bfloat16 [32768, 640], P('dp'), may hold values from -6 to 6
- w_query: bfloat16 [640, 1024], P(None, 'tensor'), may hold values from -0.25 to 0.25
- w_key: bfloat16 [640, 256], replicated, may hold values from -0.25 to 0.25
- w_value: bfloat16 [640, 256], replicated, may hold values from -0.25 to 0.25
- w_out: bfloat16 [1024, 640], P('tensor'), may hold values from -0.1875 to 0.1875
- w_gate: bfloat16 [640, 2048], P(None, 'tensor'), may hold values from -0.25 to 0.25
- w_up: bfloat16 [640, 2048], P(None, 'tensor'), may hold values from -0.25 to 0.25
- w_down: bfloat16 [2048, 640], P('tensor'), may hold values from -0.125 to 0.125
- g_attn_in: float32 [640], replicated, may hold values from 0.1 to 1.9
- g_attn_out: float32 [640], replicated, may hold values from 0.1 to 1.9
- g_ffn_in: float32 [640], replicated, may hold values from 0.1 to 1.9
- g_ffn_out: float32 [640], replicated, may hold values from 0.1 to 1.9
- g_query: float32 [256], replicated, may hold values from 0.1 to 1.9
- g_key: float32 [256], replicated, may hold values from 0.1 to 1.9
Outputs:
- output: bfloat16 [32768, 640], P('dp')
- input_grad: bfloat16 [32768, 640], P('dp')
- grad_query: float32 [640, 1024], P(None, 'tensor')
- grad_key: float32 [640, 256], replicated
- grad_value: float32 [640, 256], replicated
- grad_out: float32 [1024, 640], P('tensor')
- grad_gate: float32 [640, 2048], P(None, 'tensor')
- grad_up: float32 [640, 2048], P(None, 'tensor')
- grad_down: float32 [2048, 640], P('tensor')
- grad_attn_in: float32 [640], replicated
- grad_attn_out: float32 [640], replicated
- grad_ffn_in: float32 [640], replicated
- grad_ffn_out: float32 [640], replicated
- grad_qnorm: float32 [256], replicated
- grad_knorm: float32 [256], replicated
Inputs may be any that keep to these rules, and one draw needn't show every extreme that they name: `segments`: document numbers never fall along the tokens; a document holds at most 2048 tokens.
All inputs are finite; a program needn't handle non-finite values.
Results may differ from a plain program's by a relative error of at most 0.03.
Values may be sent and summed in bfloat16 or wider, within the bound.
A program may use at most 128 MiB of HBM per device.

v0:
```python
import math
import jax
import jax.numpy as jnp
from jax import lax
from jax.sharding import PartitionSpec as P

WINDOW = 512
LENGTH = 1024
EPSILON = 1e-06
ROPE_BASE = 10000.0
NEG_LARGE = -1e30


def in_blocks(x, dim, size):
    before, after = (x.shape[:dim], x.shape[dim + 1 :])
    return jnp.moveaxis(x.reshape(*before, size, -1, *after), dim, 0)


def sum_at_owner(x, axis, dim):
    size = lax.axis_size(axis)
    tiles = lax.all_to_all(in_blocks(x, dim, size), axis, 0, 0, tiled=True)
    return jnp.sum(tiles.astype(jnp.float32), axis=0)


def in_order(tiles, dim):
    tiles = jnp.moveaxis(tiles, 0, dim)
    lengths = tiles.shape
    return tiles.reshape(*lengths[:dim], lengths[dim] * lengths[dim + 1], *lengths[dim + 2 :])


def copy_for_each(x, axis):
    copies = jnp.broadcast_to(x, (lax.axis_size(axis), *x.shape))
    return lax.all_to_all(copies, axis, split_axis=0, concat_axis=0, tiled=True)


def collect(x, axis, dim):
    return in_order(copy_for_each(x, axis), dim)


def in_one_piece(arrays, axis, dim, along):
    both = jnp.concatenate(arrays, axis=along)
    out, at, gathered = (lax.all_gather(both, axis, axis=dim, tiled=True), 0, [])
    for a in arrays:
        gathered.append(lax.slice_in_dim(out, at, at + a.shape[along], axis=along))
        at += a.shape[along]
    return tuple(gathered)


def rms_scale(values, gain_vec):
    return (
        values * lax.rsqrt(jnp.mean(values * values, axis=-1, keepdims=True) + EPSILON) * gain_vec
    )


def gain_term(values, grad_vec):
    scaled = values * lax.rsqrt(jnp.mean(values * values, axis=-1, keepdims=True) + EPSILON)
    return jnp.sum(grad_vec * scaled, axis=0)


def rope_tables(positions, head_size):
    half_size = head_size // 2
    inv_freq = ROPE_BASE ** (-2.0 * jnp.arange(half_size, dtype=jnp.float32) / head_size)
    angles = positions.astype(jnp.float32)[:, None] * inv_freq[None, :]
    return (jnp.cos(angles), jnp.sin(angles))


def rotate(values, cosine, sine_table):
    half_size = values.shape[-1] // 2
    first_half = values[..., :half_size]
    second_half = values[..., half_size:]
    return jnp.concatenate(
        [
            first_half * cosine - second_half * sine_table,
            second_half * cosine + first_half * sine_table,
        ],
        axis=-1,
    )


def rotary_norm(raw_vec, gain_vec, cosine, sine_table):
    return rotate(rms_scale(raw_vec, gain_vec), cosine, sine_table)


def windows(blocks, fill_value):
    earlier = jnp.concatenate([jnp.full_like(blocks[:, :1], fill_value), blocks[:, :-1]], axis=1)
    return jnp.concatenate([earlier, blocks], axis=2)


def unwindow(grads, width):
    front_half = grads[:, :, :width]
    back_half = grads[:, :, width:]
    shifted = jnp.concatenate([front_half[:, 1:], jnp.zeros_like(front_half[:, :1])], axis=1)
    return back_half + shifted


def allowed_mask(seg_rows, seg_keys, width):
    row_ids = lax.broadcasted_iota(jnp.int32, (width, 2 * width), 0)
    key_ids = lax.broadcasted_iota(jnp.int32, (width, 2 * width), 1)
    in_window = (key_ids > row_ids) & (key_ids <= row_ids + width)
    return in_window & (seg_rows[:, None] == seg_keys[None, :])


def block_forward(block_item, score_scale):
    q_block, k_window, v_window, seg_rows, seg_keys = block_item
    width = q_block.shape[1]
    scores = (
        jnp.einsum("hqd,kd->hqk", q_block, k_window, preferred_element_type=jnp.float32)
        * score_scale
    )
    allowed = allowed_mask(seg_rows, seg_keys, width)[None]
    masked = jnp.where(allowed, scores, NEG_LARGE)
    row_max = jnp.max(masked, axis=-1, keepdims=True)
    expo_terms = jnp.where(allowed, jnp.exp(masked - row_max), 0.0)
    row_total = jnp.sum(expo_terms, axis=-1, keepdims=True)
    prob_low = (expo_terms / row_total).astype(jnp.bfloat16)
    block_out = jnp.einsum("hqk,kd->hqd", prob_low, v_window, preferred_element_type=jnp.float32)
    return (block_out, (row_max + jnp.log(row_total))[..., 0])


def block_backward(block_item, score_scale):
    q_block, k_window, v_window, seg_rows, seg_keys, log_totals, grad_block = block_item
    width = q_block.shape[1]
    scores = (
        jnp.einsum("hqd,kd->hqk", q_block, k_window, preferred_element_type=jnp.float32)
        * score_scale
    )
    allowed = allowed_mask(seg_rows, seg_keys, width)[None]
    prob_full = jnp.where(allowed, jnp.exp(scores - log_totals[..., None]), 0.0)
    grad_prob = jnp.einsum("hqd,kd->hqk", grad_block, v_window, preferred_element_type=jnp.float32)
    row_dot = jnp.sum(prob_full * grad_prob, axis=-1, keepdims=True)
    grad_scores = (prob_full * (grad_prob - row_dot)).astype(jnp.bfloat16)
    grad_q = (
        jnp.einsum("hqk,kd->hqd", grad_scores, k_window, preferred_element_type=jnp.float32)
        * score_scale
    )
    grad_k = (
        jnp.einsum("hqk,hqd->kd", grad_scores, q_block, preferred_element_type=jnp.float32)
        * score_scale
    )
    grad_v = jnp.einsum(
        "hqk,hqd->kd",
        prob_full.astype(jnp.bfloat16),
        grad_block,
        preferred_element_type=jnp.float32,
    )
    return (grad_q, grad_k, grad_v)


def local(
    inputs,
    segments,
    positions,
    cotangent,
    w_query,
    w_key,
    w_value,
    w_out,
    w_gate,
    w_up,
    w_down,
    g_attn_in,
    g_attn_out,
    g_ffn_in,
    g_ffn_out,
    g_query,
    g_key,
):
    row_count = inputs.shape[0]
    head_size = w_key.shape[1]
    heads_here = w_query.shape[1] // head_size
    seqs_here = row_count // LENGTH
    blocks_per = LENGTH // WINDOW
    block_total = seqs_here * blocks_per
    score_scale = 1.0 / math.sqrt(head_size)
    share_rows = row_count // lax.axis_size("tensor")
    first_row = lax.axis_index("tensor") * share_rows

    def my_rows(values):
        return lax.dynamic_slice_in_dim(values, first_row, share_rows, 0)

    whole_x = inputs.astype(jnp.float32)
    normed = rms_scale(whole_x, g_attn_in).astype(jnp.bfloat16)
    query_raw = jnp.dot(normed, w_query, preferred_element_type=jnp.float32)
    key_raw = jnp.dot(normed, w_key, preferred_element_type=jnp.float32)
    value_raw = jnp.dot(normed, w_value, preferred_element_type=jnp.float32)
    cosine, sine_table = rope_tables(positions, head_size)
    query_heads = query_raw.reshape(row_count, heads_here, head_size).transpose(1, 0, 2)
    q_rot, q_pull = jax.vjp(
        lambda raw_vec, gain_vec: rotary_norm(raw_vec, gain_vec, cosine, sine_table),
        query_heads,
        g_query,
    )
    k_rot, k_pull = jax.vjp(
        lambda raw_vec, gain_vec: rotary_norm(raw_vec, gain_vec, cosine, sine_table), key_raw, g_key
    )
    q_blocks = (
        q_rot.astype(jnp.bfloat16)
        .reshape(heads_here, block_total, WINDOW, head_size)
        .transpose(1, 0, 2, 3)
    )
    k_windows = windows(
        k_rot.astype(jnp.bfloat16).reshape(seqs_here, blocks_per, WINDOW, head_size), 0
    ).reshape(block_total, 2 * WINDOW, head_size)
    v_windows = windows(
        value_raw.astype(jnp.bfloat16).reshape(seqs_here, blocks_per, WINDOW, head_size), 0
    ).reshape(block_total, 2 * WINDOW, head_size)
    seg_rows = segments.reshape(block_total, WINDOW)
    seg_keys = windows(segments.reshape(seqs_here, blocks_per, WINDOW), -1).reshape(
        block_total, 2 * WINDOW
    )
    block_items = (q_blocks, k_windows, v_windows, seg_rows, seg_keys)
    heads_out, log_totals = lax.map(
        lambda block_item: block_forward(block_item, score_scale), block_items
    )
    heads_low = (
        heads_out.astype(jnp.bfloat16)
        .transpose(0, 2, 1, 3)
        .reshape(row_count, heads_here * head_size)
    )
    attn_term = jnp.dot(heads_low, w_out, preferred_element_type=jnp.float32)
    attn_sum = sum_at_owner(attn_term.astype(jnp.bfloat16), "tensor", 0)
    x_rows = my_rows(whole_x)
    attn_norm, attn_pull = jax.vjp(lambda values: rms_scale(values, g_attn_out), attn_sum)
    mid_rows = x_rows + attn_norm
    ffn_in, ffn_pull = jax.vjp(lambda values: rms_scale(values, g_ffn_in), mid_rows)
    ffn_low = collect(ffn_in.astype(jnp.bfloat16), "tensor", 0)
    gate_raw = jnp.dot(ffn_low, w_gate, preferred_element_type=jnp.float32)
    up_raw = jnp.dot(ffn_low, w_up, preferred_element_type=jnp.float32)
    hidden_full, act_pull = jax.vjp(
        lambda gate_in, up_in: jax.nn.gelu(gate_in, approximate=True) * up_in, gate_raw, up_raw
    )
    hidden = hidden_full.astype(jnp.bfloat16)
    ffn_term = jnp.dot(hidden, w_down, preferred_element_type=jnp.float32)
    ffn_sum = sum_at_owner(ffn_term.astype(jnp.bfloat16), "tensor", 0)
    cot_rows = my_rows(cotangent).astype(jnp.float32)
    out_norm, out_pull = jax.vjp(lambda values: rms_scale(values, g_ffn_out), ffn_sum)
    result = mid_rows + out_norm
    grad_ffn = out_pull(cot_rows)[0]
    output, grad_ffn_low = in_one_piece(
        (result.astype(jnp.bfloat16), grad_ffn.astype(jnp.bfloat16)), "tensor", 0, 1
    )
    grad_hidden = jnp.einsum("rd,fd->rf", grad_ffn_low, w_down, preferred_element_type=jnp.float32)
    grad_down = jnp.einsum("rf,rd->fd", hidden, grad_ffn_low, preferred_element_type=jnp.float32)
    grad_gate_full, grad_up_full = act_pull(grad_hidden)
    grad_gate_low = grad_gate_full.astype(jnp.bfloat16)
    grad_up_low = grad_up_full.astype(jnp.bfloat16)
    grad_gate = jnp.einsum("rd,rf->df", ffn_low, grad_gate_low, preferred_element_type=jnp.float32)
    grad_up = jnp.einsum("rd,rf->df", ffn_low, grad_up_low, preferred_element_type=jnp.float32)
    ffn_in_term = jnp.einsum(
        "rf,df->rd", grad_gate_low, w_gate, preferred_element_type=jnp.float32
    ) + jnp.einsum("rf,df->rd", grad_up_low, w_up, preferred_element_type=jnp.float32)
    ffn_in_grad = sum_at_owner(ffn_in_term.astype(jnp.bfloat16), "tensor", 0)
    grad_mid = cot_rows + ffn_pull(ffn_in_grad)[0]
    grad_attn = attn_pull(grad_mid)[0]
    grad_attn_low = collect(grad_attn.astype(jnp.bfloat16), "tensor", 0)
    grad_out = jnp.einsum("rh,rd->hd", heads_low, grad_attn_low, preferred_element_type=jnp.float32)
    grad_heads = jnp.einsum(
        "rd,hd->rh", grad_attn_low, w_out, preferred_element_type=jnp.float32
    ).astype(jnp.bfloat16)
    grad_blocks = grad_heads.reshape(block_total, WINDOW, heads_here, head_size).transpose(
        0, 2, 1, 3
    )
    grad_qb, grad_kw, grad_vw = lax.map(
        lambda block_item: block_backward(block_item, score_scale),
        block_items + (log_totals, grad_blocks),
    )
    grad_q_rot = grad_qb.transpose(1, 0, 2, 3).reshape(heads_here, row_count, head_size)
    grad_k_rot = unwindow(
        grad_kw.reshape(seqs_here, blocks_per, 2 * WINDOW, head_size), WINDOW
    ).reshape(row_count, head_size)
    grad_v_full = unwindow(
        grad_vw.reshape(seqs_here, blocks_per, 2 * WINDOW, head_size), WINDOW
    ).reshape(row_count, head_size)
    grad_query_raw, grad_qnorm = q_pull(grad_q_rot)
    grad_key_raw, grad_knorm = k_pull(grad_k_rot)
    grad_q_low = (
        grad_query_raw.transpose(1, 0, 2)
        .reshape(row_count, heads_here * head_size)
        .astype(jnp.bfloat16)
    )
    grad_k_low = grad_key_raw.astype(jnp.bfloat16)
    grad_v_low = grad_v_full.astype(jnp.bfloat16)
    grad_query = jnp.einsum("rd,rh->dh", normed, grad_q_low, preferred_element_type=jnp.float32)
    grad_key = jnp.einsum("rd,rh->dh", normed, grad_k_low, preferred_element_type=jnp.float32)
    grad_value = jnp.einsum("rd,rh->dh", normed, grad_v_low, preferred_element_type=jnp.float32)
    input_term = jnp.einsum("rh,dh->rd", grad_q_low, w_query, preferred_element_type=jnp.float32)
    input_term = input_term + jnp.einsum(
        "rh,dh->rd", grad_k_low, w_key, preferred_element_type=jnp.float32
    )
    input_term = input_term + jnp.einsum(
        "rh,dh->rd", grad_v_low, w_value, preferred_element_type=jnp.float32
    )
    input_sum = sum_at_owner(input_term.astype(jnp.bfloat16), "tensor", 0)
    x_grad_norm = jax.vjp(lambda values: rms_scale(values, g_attn_in), x_rows)[1](input_sum)[0]
    grad_rows = grad_mid + x_grad_norm
    gain_inputs = (x_rows, input_sum, attn_sum, grad_mid, mid_rows, ffn_in_grad, ffn_sum, cot_rows)
    input_grad = collect(grad_rows.astype(jnp.bfloat16), "tensor", 0)
    grad_attn_in = gain_term(gain_inputs[0], gain_inputs[1])
    grad_attn_out = gain_term(gain_inputs[2], gain_inputs[3])
    grad_ffn_in = gain_term(gain_inputs[4], gain_inputs[5])
    grad_ffn_out = gain_term(gain_inputs[6], gain_inputs[7])
    grad_query, grad_out, grad_gate, grad_up, grad_down = (
        lax.psum(grad_query.astype(jnp.bfloat16), "dp").astype(jnp.float32),
        lax.psum(grad_out.astype(jnp.bfloat16), "dp").astype(jnp.float32),
        lax.psum(grad_gate.astype(jnp.bfloat16), "dp").astype(jnp.float32),
        lax.psum(grad_up.astype(jnp.bfloat16), "dp").astype(jnp.float32),
        lax.psum(grad_down.astype(jnp.bfloat16), "dp").astype(jnp.float32),
    )
    summed_all = lax.psum(
        (
            grad_key,
            grad_value,
            grad_attn_in,
            grad_attn_out,
            grad_ffn_in,
            grad_ffn_out,
            grad_qnorm,
            grad_knorm,
        ),
        ("dp", "tensor"),
    )
    return (
        output,
        input_grad,
        grad_query,
        summed_all[0],
        summed_all[1],
        grad_out,
        grad_gate,
        grad_up,
        grad_down,
        summed_all[2],
        summed_all[3],
        summed_all[4],
        summed_all[5],
        summed_all[6],
        summed_all[7],
    )


def solution(mesh):
    placed = (
        P("dp", None),
        P("dp"),
        P("dp"),
        P("dp", None),
        P(None, "tensor"),
        P(),
        P(),
        P("tensor", None),
        P(None, "tensor"),
        P(None, "tensor"),
        P("tensor", None),
        P(),
        P(),
        P(),
        P(),
        P(),
        P(),
    )
    return jax.shard_map(
        local,
        mesh=mesh,
        in_specs=placed,
        out_specs=(
            P("dp", None),
            P("dp", None),
            P(None, "tensor"),
            P(),
            P(),
            P("tensor", None),
            P(None, "tensor"),
            P(None, "tensor"),
            P("tensor", None),
            P(),
            P(),
            P(),
            P(),
            P(),
            P(),
        ),
        check_vma=False,
    )
```

profile of v0, /device:TPU:1, one launch (start us, length us, event | category | flops | bytes accessed | tf_op | source)
XLA Modules:
  0.0 761.8 jit_solution(5090513711252032929)
XLA Ops:
  9.4 1.6 multiply_reduce_fusion.1
  11.1 2.1 convolution_convert_fusion.6
  15.2 2.4 fusion.97
  17.9 2.4 fusion.91
  20.3 1.1 fusion.60
  22.3 10.3 %while.28 = (s32[]{:T(128)}, bf16[2,1,512,256]{3,2,1,0:T(8,128)(2,1)S(1)}, f32[2,1,512]{2,1,0:T(1,128)}, s32[2,512]{1,0:T(2,128)S(1)}, s32[2,1024]{1,0:T(2,128)S...) while((s32[]{:T(128)}, ...), condition=%wide.region_6.7_spmd.clone, body=%wide.region_3.6_spmd.sunk.clone | while | flops 552075264 | bytes 8220833 | solution.py:212
  22.3 2.0 fusion.189
  24.3 1.0 fusion.190
  25.3 1.4 fusion.191
  27.5 2.0 fusion.189
  29.5 1.0 fusion.190
  30.5 1.4 fusion.191
  32.6 2.6 convolution_convert_fusion
  35.2 5.7 all-to-all-start
  40.9 1.6 convert_element_type.144
  42.5 14.9 %all-to-all-done = bf16[4,256,640]{2,1,0:T(8,128)(2,1)} async-done(((bf16[4,256,640]{2,1,0:T(8,128)(2,1)}), bf16[4,256,640]{2,1,0:T(8,128)(2,1)}, u32[]{:S(2)}, u32[]{:S(2)}) %all-to-all-start) | async-done | bytes 1310752 | tf_op jit(solution)/shard_map/all_to_all | solution.py:21
  57.4 1.6 convert_reduce_fusion.3
  59.6 2.0 multiply_reduce_fusion.14
  62.4 19.7 %all_to_all.35 = bf16[4,256,640]{2,1,0:T(8,128)(2,1)S(1)} all-to-all(bf16[4,256,640]{2,1,0:T(8,128)(2,1)S(1)} %broadcast_in_dim.57), channel_id=1, replica_groups=mesh['dp'=32,'tensor'=4] {'tensor'}, dimensions={0} | all-to-all | bytes 2621440 | tf_op jit(solution)/shard_map/all_to_all | solution.py:33
  83.7 2.6 multiply_convert_fusion.3
  87.3 19.8 %all_to_all.36 = bf16[4,256,640]{2,1,0:T(8,128)(2,1)S(1)} all-to-all(bf16[4,256,640]{2,1,0:T(8,128)(2,1)S(1)} %bitcast.223), channel_id=1, replica_groups=mesh['dp'=32,'tensor'=4] {'tensor'}, dimensions={0} | all-to-all | bytes 2621440 | tf_op jit(solution)/shard_map/all_to_all | solution.py:21
  109.6 36.9 %all-gather.2.cloned.1.call-done = bf16[1024,1280]{1,0:T(8,128)(2,1)} async-done(((bf16[256,1280]{1,0:T(8,128)(2,1)}), bf16[1024,1280]{1,0:T(8,128)(2,1)}) %all-gather.2.cloned.1.call-update) | async-done | bytes 2621456 | tf_op jit(solution)/shard_map/all_gather | solution.py:42
  146.5 5.0 multiply_convert_fusion.2
  154.2 18.6 %all_to_all.37 = bf16[4,256,640]{2,1,0:T(8,128)(2,1)S(1)} all-to-all(bf16[4,256,640]{2,1,0:T(8,128)(2,1)S(1)} %bitcast.209), channel_id=1, replica_groups=mesh['dp'=32,'tensor'=4] {'tensor'}, dimensions={0} | all-to-all | bytes 2621440 | tf_op jit(solution)/shard_map/all_to_all | solution.py:21
  173.9 2.0 multiply_reduce_fusion.7
  176.1 1.2 broadcast_in_dim.61
  177.3 5.3 all-to-all-start.4
  182.6 3.0 convolution_convert_fusion.3
  185.6 1.7 convolution_convert_fusion.4
  187.9 1.9 convolution_convert_fusion.2
  189.8 9.4 %all-to-all-done.4 = bf16[4,256,640]{2,1,0:T(8,128)(2,1)} async-done(((bf16[4,256,640]{2,1,0:T(8,128)(2,1)}), bf16[4,256,640]{2,1,0:T(8,128)(2,1)}, u32[]{:S(2)}, u32[]{:S(2)}) %all-to-all-start.4) | async-done | bytes 1310752 | tf_op jit(solution)/shard_map/all_to_all | solution.py:33
  199.1 2.7 convolution_convert_fusion.7
  201.9 2.0 convolution_convert_fusion.5
  203.9 15.6 %while.29 = (s32[]{:T(128)}, f32[2,1,512,256]{3,2,1,0:T(8,128)S(1)}, f32[2,1024,256]{2,1,0:T(8,128)}, f32[2,1024,256]{2,1,0:T(8,128)}, s32[2,512]{1,0:T(2,128)S(...) while((s32[]{:T(128)}, ...), condition=%wide.region_18.19_spmd.clone, body=%wide.region_16.18_spmd.sunk.clone | while | flops 1349910528 | bytes 58758412 | solution.py:263
  205.4 1.2 multiply_reduce_fusion.18
  206.8 1.3 copy-done.18
  210.5 1.3 copy-done.22
  213.0 1.2 multiply_reduce_fusion.18
  214.4 1.3 copy-done.18
  218.2 1.3 copy-done.22
  219.5 2.3 fusion.94
  223.5 1.5 convolution_convert_fusion.8
  225.1 1.8 fusion.118
  226.9 1.2 slice.67
  229.2 2.3 fusion.100
  233.1 2.1 fusion.119
  236.3 3.5 add_convert_fusion
  239.8 5.4 all-to-all-start.5
  245.2 18.8 %all-to-all-done.5 = bf16[4,256,640]{2,1,0:T(8,128)(2,1)} async-done(((bf16[4,256,640]{2,1,0:T(8,128)(2,1)}), bf16[4,256,640]{2,1,0:T(8,128)(2,1)}, u32[]{:S(2)}, u32[]{:S(2)}) %all-to-all-start.5) | async-done | bytes 1310752 | tf_op jit(solution)/shard_map/all_to_all | solution.py:21
  264.1 1.6 convert_reduce_fusion
  266.2 1.2 broadcast_in_dim.101
  267.4 4.1 all-to-all-start.6
  271.5 2.7 fusion.113
  274.2 1.6 fusion.112
  275.8 2.5 slice.62
  278.3 71.3 %all-reduce.9 = (f32[640]{0:T(1024)}, f32[640]{0:T(1024)}, f32[640]{0:T(1024)}, f32[640]{0:T(1024)}, f32[256]{0:T(256)}, /*index=5*/f32[256]{0:T(256)}) all-reduce(f32[640]{0:T(1024)S(1)} %get-tuple-element.133, f32[640]{0:T(1024)S(1)} %copy-done.65, f32[640]{0:T(1024)S(1)} %copy-done.64, ...), channel_id=1, replica_groups=mesh['dp'=32,'tensor'=4] {'dp','tensor'}, use_global_device_ids=true, to_apply=%region_32.33 | all-reduce | flops 3072 | bytes 24576 | tf_op jit(solution)/shard_map/psum | solution.py:309
  349.6 226.8 %all-reduce.17.cloned.1.call-done = (bf16[640,256]{1,0:T(8,128)(2,1)}, bf16[256,640]{1,0:T(8,128)(2,1)}, bf16[640,512]{1,0:T(8,128)(2,1)}, bf16[640,512]{1,0:T(8,128)(2,1)}, bf16[512,640]{1,0:T(8,128)(2,1)}) async-done(((bf16[640,256]{1,0:T(8,128)(2,1)}, bf16[256,640]{1,0:T(8,128)(2,1)}, bf16[640,512]{1,0:T(8,128)(2,1)}, bf16[640,512]{1,0:T(8,128)(2,1)}, bf16[512,640]{1,0:T(8,128)(2,1)}), ...) | async-done | bytes 2621456 | tf_op jit(solution)/shard_map/psum | solution.py:303
  576.4 2.0 convert_element_type.173
  578.4 1.9 convert_element_type.175
  580.2 1.2 convert_element_type.177
  581.4 1.2 convert_element_type.179
  582.7 1.1 convert_element_type.181
  583.8 168.3 %all-reduce.15.cloned.1.call-done = (f32[640,256]{1,0:T(8,128)}, f32[640,256]{1,0:T(8,128)}) async-done(((f32[640,256]{1,0:T(8,128)}, f32[640,256]{1,0:T(8,128)}), (f32[640,256]{1,0:T(8,128)}, f32[640,256]{1,0:T(8,128)})) %all-reduce.15.cloned.1.call-update) | async-done | bytes 1310736 | tf_op jit(solution)/shard_map/psum | solution.py:309
  752.1 1.1 copy.71
  (274 shorter events, 32.9 us)
Async XLA Ops:
  7.2 79.1 %copy-start = (bf16[512,640]{1,0:T(8,128)(2,1)S(1)}, bf16[512,640]{1,0:T(8,128)(2,1)}, u32[]{:S(2)}) copy-start(bf16[512,640]{1,0:T(8,128)(2,1)} %param.31) | copy-start | bytes 1966084
  7.2 10.6 %copy-start.79 = (f32[128]{0:T(128)}, f32[128]{0:T(128)S(1)}, u32[]{:S(2)}) copy-start(f32[128]{0:T(128)S(1)} %multiply_power_fusion) | copy-start | bytes 1540
  11.1 2.2 copy-start.9
  11.1 2.2 copy-start.44
  11.1 2.2 copy-start.61
  11.1 3.0 copy-start.81
  14.9 2.7 copy-start.68
  14.9 2.9 copy-start.4
  15.0 2.7 copy-start.70
  15.0 2.6 copy-start.48
  35.2 22.2 %all-to-all-start = ((bf16[4,256,640]{2,1,0:T(8,128)(2,1)}), bf16[4,256,640]{2,1,0:T(8,128)(2,1)}, u32[]{:S(2)}, u32[]{:S(2)}) async-start(bf16[4,256,640]{2,1,0:T(8,128)(2,1)} %bitcast.29), calls=%async_computation | async-start | bytes 2621440 | tf_op jit(solution)/shard_map/all_to_all | solution.py:21
  40.9 105.6 %all-gather.2.cloned.1.call-start = ((), (), s32[]{:S(2)}) async-start(), calls=%async_computation.7 | async-start | bytes 3276800 | tf_op jit(solution)/shard_map/all_gather | solution.py:42
  57.4 4.8 copy-start.50
  59.6 2.0 copy-start.56
  62.3 19.8 %copy-start.36 = (bf16[640,512]{1,0:T(8,128)(2,1)S(1)}, bf16[640,512]{1,0:T(8,128)(2,1)}, u32[]{:S(2)}) copy-start(bf16[640,512]{1,0:T(8,128)(2,1)} %param.29) | copy-start | bytes 1966084
  83.7 2.6 copy-start.83
  86.3 20.9 %copy-start.84 = (bf16[1024,512]{1,0:T(8,128)(2,1)}, bf16[1024,512]{1,0:T(8,128)(2,1)S(1)}, u32[]{:S(2)}) copy-start(bf16[1024,512]{1,0:T(8,128)(2,1)S(1)} %get-tuple-element.220) | copy-start | bytes 3145732
  87.3 20.2 %copy-start.29 = (bf16[1024,640]{1,0:T(8,128)(2,1)S(1)}, bf16[1024,640]{1,0:T(8,128)(2,1)}, u32[]{:S(2)}) copy-start(bf16[1024,640]{1,0:T(8,128)(2,1)} %param.24) | copy-start | bytes 3932164
  87.3 20.2 %copy-start.60 = (f32[640]{0:T(1024)S(1)}, f32[640]{0:T(1024)}, u32[]{:S(2)}) copy-start(f32[640]{0:T(1024)} %param.35) | copy-start | bytes 7684
  146.5 5.1 copy-start.37
  154.2 18.9 %copy-start.51 = (f32[640]{0:T(1024)S(1)}, f32[640]{0:T(1024)}, u32[]{:S(2)}) copy-start(f32[640]{0:T(1024)} %param.34) | copy-start | bytes 7684
  154.2 18.9 %copy-start.59 = (f32[256]{0:T(256)S(1)}, f32[256]{0:T(256)}, u32[]{:S(2)}) copy-start(f32[256]{0:T(256)} %copy-done.58) | copy-start | bytes 3076
  173.1 2.9 copy-start.76
  176.1 6.5 copy-start.17
  177.3 21.8 %all-to-all-start.4 = ((bf16[4,256,640]{2,1,0:T(8,128)(2,1)}), bf16[4,256,640]{2,1,0:T(8,128)(2,1)}, u32[]{:S(2)}, u32[]{:S(2)}) async-start(bf16[4,256,640]{2,1,0:T(8,128)(2,1)} %broadcast_in_dim.61), calls=%async_computation.4 | async-start | bytes 2621440 | tf_op jit(solution)/shard_map/all_to_all | solution.py:33
  182.6 393.8 %all-reduce.17.cloned.1.call-start = ((), (), s32[]{:S(2)}) async-start(), calls=%async_computation.9 | async-start | bytes 5242880 | tf_op jit(solution)/shard_map/psum | solution.py:303
  182.6 3.0 copy-start.27
  185.6 1.7 copy-start.30
  185.6 2.2 copy-start.85
  199.1 2.8 copy-start.41
  199.1 4.7 copy-start.24
  199.1 4.8 copy-start.55
  201.9 2.0 copy-start.40
  203.9 15.6 %copy-start.80 = (f32[128]{0:T(128)S(1)}, f32[128]{0:T(128)}, u32[]{:S(2)}) copy-start(f32[128]{0:T(128)} %copy-done.79) | copy-start | bytes 1540
  208.1 1.9 copy-start.21
  208.6 1.8 copy-start.19
  215.8 1.9 copy-start.21
  216.3 1.8 copy-start.19
  219.5 2.3 copy-start.5
  219.5 2.3 copy-start.49
  219.5 2.3 copy-start.71
  219.5 2.8 copy-start.69
  225.1 3.0 copy-start.20
  226.9 2.1 copy-start.23
  229.0 2.4 copy-start.3
  229.0 2.4 copy-start.47
  229.0 2.4 copy-start.73
  229.1 2.8 copy-start.67
  239.8 5.4 copy-start.74
  239.8 25.9 %copy-start.6 = (f32[1024,640]{1,0:T(8,128)S(1)}, f32[1024,640]{1,0:T(8,128)}, u32[]{:S(2)}) copy-start(f32[1024,640]{1,0:T(8,128)} %convert_element_type.144) | copy-start | bytes 7864324
  239.8 24.3 %all-to-all-start.5 = ((bf16[4,256,640]{2,1,0:T(8,128)(2,1)}), bf16[4,256,640]{2,1,0:T(8,128)(2,1)}, u32[]{:S(2)}, u32[]{:S(2)}) async-start(bf16[4,256,640]{2,1,0:T(8,128)(2,1)} %bitcast.207), calls=%async_computation.5 | async-start | bytes 2621440 | tf_op jit(solution)/shard_map/all_to_all | solution.py:21
  245.2 20.7 %copy-start.8 = (f32[256,640]{1,0:T(8,128)S(1)}, f32[256,640]{1,0:T(8,128)}, u32[]{:S(2)}) copy-start(f32[256,640]{1,0:T(8,128)} %copy-done.7) | copy-start | bytes 1966084
  266.2 5.3 copy-start.11
  267.4 82.3 %all-to-all-start.6 = ((bf16[4,256,640]{2,1,0:T(8,128)(2,1)}), bf16[4,256,640]{2,1,0:T(8,128)(2,1)S(1)}, u32[]{:S(2)}, u32[]{:S(2)}) async-start(bf16[4,256,640]{2,1,0:T(8,128)(2,1)} %broadcast_in_dim.101), calls=%async_computation.6 | async-start | bytes 2621440 | tf_op jit(solution)/shard_map/all_to_all | solution.py:33
  271.5 2.7 copy-start.13
  271.5 480.7 %all-reduce.15.cloned.1.call-start = ((), (), s32[]{:S(2)}) async-start(), calls=%async_computation.8 | async-start | bytes 2621440 | tf_op jit(solution)/shard_map/psum | solution.py:309
  275.7 2.5 copy-start.63
  275.7 2.5 copy-start.64
  275.7 2.5 copy-start.65
  576.4 3.8 copy-start.35
  576.4 5.0 copy-start.34
  580.2 2.5 copy-start.33
  752.1 2.4 copy-start.31
  752.1 3.2 copy-start.1
  (36 other events, 43.0 us)
Sparse Core Ops, SparseCore 0:
  109.7 36.6 all-gather.1
  235.4 340.9 all-reduce.16
  581.9 170.1 all-reduce.14
where the time goes:
time: 763 us; the launch traced here: 762 us
  waiting for transfers between devices  475 us (62%)
  blocking collectives  129 us (17%)
  matrix products  55.3 us (7%)
  other arithmetic  39.8 us (5%)
  local copies, waits for them, and re-layouts  26.5 us (3%)
  starting transfers between devices  20.5 us (3%)
  between operations  14.7 us (2%)
    psum x1, waiting for transfers between devices, local(): lax.psum(grad_query.astype(jnp.bfloat16), 'dp').astype(jnp.float32)  227 us
    psum x1, waiting for transfers between devices, local(): lax.psum((grad_key, grad_value, grad_attn_in, grad_attn_out, grad_ffn_in,...  168 us
    psum x1, blocking collectives, local(): lax.psum((grad_key, grad_value, grad_attn_in, grad_attn_out, grad_ffn_in,...  71.3 us
    all_to_all x2, blocking collectives, sum_at_owner(): tiles = lax.all_to_all(in_blocks(x, dim, size), axis, 0, 0, tiled=True)  38.5 us
    all_gather x1, waiting for transfers between devices, in_one_piece(): lax.all_gather(both, axis, axis=dim, tiled=True)  36.9 us
    all_to_all x2, waiting for transfers between devices, sum_at_owner(): tiles = lax.all_to_all(in_blocks(x, dim, size), axis, 0, 0, tiled=True)  33.7 us
    all_to_all x1, blocking collectives, copy_for_each(): return lax.all_to_all(copies, axis, split_axis=0, concat_axis=0, tiled=True)  19.7 us
  transfers between devices with their start and end apart: 7, of which 6 were waited for; matrix products, arithmetic and copies ran while one was open for 4% of the time, Pallas kernels for 0%

commit v1 on v0

--- a/solution.py
+++ b/solution.py
@@ -307,17 +307,20 @@
         lax.psum(grad_down.astype(jnp.bfloat16), "dp").astype(jnp.float32),
     )
     summed_all = lax.psum(
-        (
-            grad_key,
-            grad_value,
-            grad_attn_in,
-            grad_attn_out,
-            grad_ffn_in,
-            grad_ffn_out,
-            grad_qnorm,
-            grad_knorm,
+        lax.psum(
+            (
+                grad_key,
+                grad_value,
+                grad_attn_in,
+                grad_attn_out,
+                grad_ffn_in,
+                grad_ffn_out,
+                grad_qnorm,
+                grad_knorm,
+            ),
+            "tensor",
         ),
-        ("dp", "tensor"),
+        "dp",
     )
     return (
         output,

time: 763 us -> 1010 us (1.32)
  the two profiles are of different devices: /device:TPU:1 before, /device:TPU:0 now
where the time goes in v1:
time: 1010 us
  waiting for transfers between devices  587 us (58%)
  blocking collectives  266 us (26%)
  matrix products  48.7 us (5%)
  other arithmetic  42.8 us (4%)
  local copies, waits for them, and re-layouts  29.6 us (3%)
  starting transfers between devices  16.5 us (2%)
  between operations  14.7 us (1%)
    psum x1, waiting for transfers between devices, local(): lax.psum(lax.psum((grad_key, grad_value, grad_attn_in, grad_attn_out, gra...  350 us
    psum x1, blocking collectives, local(): lax.psum(lax.psum((grad_key, grad_value, grad_attn_in, grad_attn_out, gra...  184 us
    psum x1, waiting for transfers between devices, local(): lax.psum(grad_query.astype(jnp.bfloat16), 'dp').astype(jnp.float32)  150 us
    all_to_all x2, blocking collectives, sum_at_owner(): tiles = lax.all_to_all(in_blocks(x, dim, size), axis, 0, 0, tiled=True)  39.5 us
    all_gather x1, waiting for transfers between devices, in_one_piece(): lax.all_gather(both, axis, axis=dim, tiled=True)  35.8 us
    all_to_all x2, waiting for transfers between devices, sum_at_owner(): tiles = lax.all_to_all(in_blocks(x, dim, size), axis, 0, 0, tiled=True)  34 us
    psum x1, blocking collectives, local(): lax.psum((grad_key, grad_value, grad_attn_in, grad_attn_out, grad_ffn_in,...  22.4 us
  transfers between devices with their start and end apart: 8, of which 7 were waited for; matrix products, arithmetic and copies ran while one was open for 3% of the time, Pallas kernels for 0%

profile of v1, /device:TPU:0, one launch (start us, length us, event | category | flops | bytes accessed | tf_op | source)
XLA Modules:
  0.0 1005.5 jit_solution(3654294271253626096)
XLA Ops:
  9.4 1.6 multiply_reduce_fusion.1
  11.1 2.1 convolution_convert_fusion.6
  16.2 2.4 fusion.97
  18.8 2.4 fusion.91
  21.2 1.1 fusion.60
  23.2 10.3 %while.28 = (s32[]{:T(128)}, bf16[2,1,512,256]{3,2,1,0:T(8,128)(2,1)S(1)}, f32[2,1,512]{2,1,0:T(1,128)}, s32[2,512]{1,0:T(2,128)S(1)}, s32[2,1024]{1,0:T(2,128)S...) while((s32[]{:T(128)}, ...), condition=%wide.region_6.7_spmd.clone, body=%wide.region_3.6_spmd.sunk.clone | while | flops 552075264 | bytes 8220833 | solution.py:212
  23.2 2.0 fusion.189
  26.2 1.4 fusion.191
  28.4 2.0 fusion.189
  31.4 1.4 fusion.191
  33.5 2.8 convolution_convert_fusion
  36.3 4.3 all-to-all-start
  40.7 1.7 convert_element_type.144
  42.3 15.6 %all-to-all-done = bf16[4,256,640]{2,1,0:T(8,128)(2,1)} async-done(((bf16[4,256,640]{2,1,0:T(8,128)(2,1)}), bf16[4,256,640]{2,1,0:T(8,128)(2,1)}, u32[]{:S(2)}, u32[]{:S(2)}) %all-to-all-start) | async-done | bytes 1310752 | tf_op jit(solution)/shard_map/all_to_all | solution.py:21
  57.9 1.6 convert_reduce_fusion.3
  59.6 2.0 multiply_reduce_fusion.14
  61.9 19.8 %all_to_all.35 = bf16[4,256,640]{2,1,0:T(8,128)(2,1)S(1)} all-to-all(bf16[4,256,640]{2,1,0:T(8,128)(2,1)S(1)} %broadcast_in_dim.57), channel_id=1, replica_groups=mesh['dp'=32,'tensor'=4] {'tensor'}, dimensions={0} | all-to-all | bytes 2621440 | tf_op jit(solution)/shard_map/all_to_all | solution.py:33
  83.3 2.6 multiply_convert_fusion.3
  86.9 19.8 %all_to_all.36 = bf16[4,256,640]{2,1,0:T(8,128)(2,1)S(1)} all-to-all(bf16[4,256,640]{2,1,0:T(8,128)(2,1)S(1)} %bitcast.225), channel_id=1, replica_groups=mesh['dp'=32,'tensor'=4] {'tensor'}, dimensions={0} | all-to-all | bytes 2621440 | tf_op jit(solution)/shard_map/all_to_all | solution.py:21
  109.2 35.8 %all-gather.2.cloned.1.call-done = bf16[1024,1280]{1,0:T(8,128)(2,1)} async-done(((bf16[256,1280]{1,0:T(8,128)(2,1)}), bf16[1024,1280]{1,0:T(8,128)(2,1)}) %all-gather.2.cloned.1.call-update) | async-done | bytes 2621456 | tf_op jit(solution)/shard_map/all_gather | solution.py:42
  145.0 5.0 multiply_convert_fusion.2
  152.7 19.7 %all_to_all.37 = bf16[4,256,640]{2,1,0:T(8,128)(2,1)S(1)} all-to-all(bf16[4,256,640]{2,1,0:T(8,128)(2,1)S(1)} %bitcast.209), channel_id=1, replica_groups=mesh['dp'=32,'tensor'=4] {'tensor'}, dimensions={0} | all-to-all | bytes 2621440 | tf_op jit(solution)/shard_map/all_to_all | solution.py:21
  173.4 2.0 multiply_reduce_fusion.7
  176.2 1.2 broadcast_in_dim.61
  177.4 3.5 all-to-all-start.4
  181.0 3.5 convolution_convert_fusion.3
  184.5 1.7 convolution_convert_fusion.4
  186.8 1.9 convolution_convert_fusion.2
  188.6 9.5 all-to-all-done.4
  198.2 1.8 convolution_convert_fusion.5
  200.0 16.4 %while.29 = (s32[]{:T(128)}, f32[2,1,512,256]{3,2,1,0:T(8,128)}, f32[2,1024,256]{2,1,0:T(8,128)}, f32[2,1024,256]{2,1,0:T(8,128)}, s32[2,512]{1,0:T(2,128)S(1)},...) while((s32[]{:T(128)}, f32[2,1,512,256]{3,2,1,0:T(8,128)}, ...), condition=%wide.region_18.19_spmd.clone, body=%wide.region_16.18_spmd.sunk.clone | while | flops 1349910528 | bytes 67147072 | solution.py:263
  201.2 1.2 multiply_reduce_fusion.18
  202.7 1.3 copy-done.22
  206.9 1.3 copy-done.25
  209.4 1.2 multiply_reduce_fusion.18
  210.8 1.3 copy-done.22
  215.1 1.3 copy-done.25
  216.4 1.2 slice.67
  217.6 1.3 fusion.61
  219.5 2.3 fusion.100
  223.1 1.6 fusion.113
  224.7 1.6 fusion.112
  226.7 3.7 fusion.94
  231.9 1.3 convolution_convert_fusion.7
  233.2 1.5 convolution_convert_fusion.8
  238.0 1.7 add_convert_fusion
  239.7 4.6 all-to-all-start.5
  244.4 18.4 %all-to-all-done.5 = bf16[4,256,640]{2,1,0:T(8,128)(2,1)} async-done(((bf16[4,256,640]{2,1,0:T(8,128)(2,1)}), bf16[4,256,640]{2,1,0:T(8,128)(2,1)}, u32[]{:S(2)}, u32[]{:S(2)}) %all-to-all-start.5) | async-done | bytes 1310752 | tf_op jit(solution)/shard_map/all_to_all | solution.py:21
  262.7 1.6 convert_reduce_fusion
  265.4 8.1 all-reduce.20.cloned.1.call-done
  273.5 1.3 fusion.89
  274.8 1.2 broadcast_in_dim.101
  276.0 3.7 all-to-all-start.6
  279.7 2.5 slice.62
  282.2 22.4 %all-reduce.11 = (f32[640]{0:T(1024)S(1)}, f32[640]{0:T(1024)S(1)}, f32[640]{0:T(1024)S(1)}, f32[640]{0:T(1024)S(1)}, f32[256]{0:T(256)S(1)}, /*index=5*/f32[256]{0:T(256)S(1)}) all-reduce(f32[640]{0:T(1024)S(1)} %get-tuple-element.133, f32[640]{0:T(1024)S(1)} %copy-done.64, ...), channel_id=1, replica_groups=mesh['dp'=32,'tensor'=4] {'tensor'}, use_global_device_ids=true, to_apply=%region_34.35 | all-reduce | flops 3072 | bytes 24576 | tf_op jit(solution)/shard_map/psum | solution.py:310
  304.6 183.8 %all-reduce.9 = (f32[640]{0:T(1024)}, f32[640]{0:T(1024)}, f32[640]{0:T(1024)}, f32[640]{0:T(1024)}, f32[256]{0:T(256)}, /*index=5*/f32[256]{0:T(256)}) all-reduce(f32[640]{0:T(1024)S(1)} %get-tuple-element.191, f32[640]{0:T(1024)S(1)} %get-tuple-element.192, ...), channel_id=1, replica_groups=mesh['dp'=32,'tensor'=4] {'dp'}, use_global_device_ids=true, to_apply=%region_35.36 | all-reduce | flops 3072 | bytes 24576 | tf_op jit(solution)/shard_map/psum | solution.py:309
  488.4 150.2 %all-reduce.22.cloned.1.call-done = (bf16[640,256]{1,0:T(8,128)(2,1)}, bf16[256,640]{1,0:T(8,128)(2,1)}, bf16[640,512]{1,0:T(8,128)(2,1)}, bf16[640,512]{1,0:T(8,128)(2,1)}, bf16[512,640]{1,0:T(8,128)(2,1)}) async-done(((bf16[640,256]{1,0:T(8,128)(2,1)}, bf16[256,640]{1,0:T(8,128)(2,1)}, bf16[640,512]{1,0:T(8,128)(2,1)}, bf16[640,512]{1,0:T(8,128)(2,1)}, bf16[512,640]{1,0:T(8,128)(2,1)}), ...) | async-done | bytes 2621456 | tf_op jit(solution)/shard_map/psum | solution.py:303
  638.6 2.0 convert_element_type.173
  640.5 1.9 convert_element_type.175
  642.4 1.2 convert_element_type.177
  643.6 1.2 convert_element_type.179
  644.9 1.1 convert_element_type.181
  646.0 349.7 %all-reduce.18.cloned.1.call-done = (f32[640,256]{1,0:T(8,128)}, f32[640,256]{1,0:T(8,128)}) async-done(((f32[640,256]{1,0:T(8,128)}, f32[640,256]{1,0:T(8,128)}), (f32[640,256]{1,0:T(8,128)}, f32[640,256]{1,0:T(8,128)})) %all-reduce.18.cloned.1.call-update) | async-done | bytes 1310736 | tf_op jit(solution)/shard_map/psum | solution.py:309
  995.8 1.1 copy.73
  (272 shorter events, 38.7 us)
Async XLA Ops:
  7.2 78.7 %copy-start = (bf16[512,640]{1,0:T(8,128)(2,1)S(1)}, bf16[512,640]{1,0:T(8,128)(2,1)}, u32[]{:S(2)}) copy-start(bf16[512,640]{1,0:T(8,128)(2,1)} %param.31) | copy-start | bytes 1966084
  7.2 11.5 %copy-start.74 = (f32[128]{0:T(128)}, f32[128]{0:T(128)S(1)}, u32[]{:S(2)}) copy-start(f32[128]{0:T(128)S(1)} %multiply_power_fusion) | copy-start | bytes 1540
  11.1 2.2 copy-start.10
  11.1 2.2 copy-start.46
  11.1 2.2 copy-start.60
  11.1 3.5 copy-start.76
  14.0 2.1 copy-start.4
  14.0 1.9 copy-start.69
  15.4 3.4 copy-start.2
  15.4 3.2 copy-start.71
  15.4 3.4 copy-start.50
  26.2 1.5 copy-start.56
  31.4 1.5 copy-start.56
  33.5 2.8 copy-start.16
  36.3 21.6 %all-to-all-start = ((bf16[4,256,640]{2,1,0:T(8,128)(2,1)}), bf16[4,256,640]{2,1,0:T(8,128)(2,1)}, u32[]{:S(2)}, u32[]{:S(2)}) async-start(bf16[4,256,640]{2,1,0:T(8,128)(2,1)} %bitcast.29), calls=%async_computation | async-start | bytes 2621440 | tf_op jit(solution)/shard_map/all_to_all | solution.py:21
  40.6 104.4 %all-gather.2.cloned.1.call-start = ((), (), s32[]{:S(2)}) async-start(), calls=%async_computation.7 | async-start | bytes 3276800 | tf_op jit(solution)/shard_map/all_gather | solution.py:42
  42.3 17.3 %copy-start.55 = (f32[640]{0:T(1024)S(1)}, f32[640]{0:T(1024)}, u32[]{:S(2)}) copy-start(f32[640]{0:T(1024)} %param.33) | copy-start | bytes 7684
  42.3 19.3 %copy-start.54 = (f32[640]{0:T(1024)S(1)}, f32[640]{0:T(1024)}, u32[]{:S(2)}) copy-start(f32[640]{0:T(1024)} %param.34) | copy-start | bytes 7684
  61.8 20.0 %copy-start.40 = (bf16[640,512]{1,0:T(8,128)(2,1)S(1)}, bf16[640,512]{1,0:T(8,128)(2,1)}, u32[]{:S(2)}) copy-start(bf16[640,512]{1,0:T(8,128)(2,1)} %param.29) | copy-start | bytes 1966084
  81.7 1.6 copy-start.42
  83.3 2.6 copy-start.78
  86.9 20.2 %copy-start.33 = (bf16[1024,640]{1,0:T(8,128)(2,1)S(1)}, bf16[1024,640]{1,0:T(8,128)(2,1)}, u32[]{:S(2)}) copy-start(bf16[1024,640]{1,0:T(8,128)(2,1)} %param.24) | copy-start | bytes 3932164
  86.9 20.2 %copy-start.59 = (f32[640]{0:T(1024)S(1)}, f32[640]{0:T(1024)}, u32[]{:S(2)}) copy-start(f32[640]{0:T(1024)} %param.35) | copy-start | bytes 7684
  145.0 5.1 copy-start.41
  150.0 1.6 copy-start.43
  177.4 20.8 %all-to-all-start.4 = ((bf16[4,256,640]{2,1,0:T(8,128)(2,1)}), bf16[4,256,640]{2,1,0:T(8,128)(2,1)S(1)}, u32[]{:S(2)}, u32[]{:S(2)}) async-start(bf16[4,256,640]{2,1,0:T(8,128)(2,1)} %broadcast_in_dim.61), calls=%async_computation.4 | async-start | bytes 2621440 | tf_op jit(solution)/shard_map/all_to_all | solution.py:33
  180.9 92.5 %all-reduce.20.cloned.1.call-start = ((), (), s32[]{:S(2)}) async-start(), calls=%async_computation.9 | async-start | bytes 2621440 | tf_op jit(solution)/shard_map/psum | solution.py:310
  181.0 3.5 copy-start.21
  181.0 3.5 copy-start.31
  184.5 1.7 copy-start.34
  184.5 2.2 copy-start.80
  188.6 11.3 %copy-start.44 = (bf16[2,1,512,256]{3,2,1,0:T(8,128)(2,1)S(1)}, bf16[2,1,512,256]{3,2,1,0:T(8,128)(2,1)}, u32[]{:S(2)}) copy-start(bf16[2,1,512,256]{3,2,1,0:T(8,128)(2,1)} %get-tuple-element.537) | copy-start | bytes 1572868
  188.6 11.4 %copy-start.58 = (f32[2,1,512]{2,1,0:T(1,128)S(1)}, f32[2,1,512]{2,1,0:T(1,128)}, u32[]{:S(2)}) copy-start(f32[2,1,512]{2,1,0:T(1,128)} %get-tuple-element.434) | copy-start | bytes 12292
  198.2 1.8 copy-start.18
  202.4 1.6 copy-start.22
  204.0 1.9 copy-start.24
  210.6 1.6 copy-start.22
  212.2 1.9 copy-start.24
  216.4 2.5 copy-start.26
  219.0 2.8 copy-start.5
  219.0 2.8 copy-start.53
  219.0 2.8 copy-start.70
  219.5 2.8 copy-start.68
  223.1 1.6 copy-start.12
  226.4 4.1 copy-start.3
  226.4 4.1 copy-start.51
  226.4 4.1 copy-start.72
  226.4 412.2 %all-reduce.22.cloned.1.call-start = ((), (), s32[]{:S(2)}) async-start(), calls=%async_computation.10 | async-start | bytes 5242880 | tf_op jit(solution)/shard_map/psum | solution.py:303
  226.7 4.3 copy-start.66
  239.7 4.6 copy-start.73
  239.7 25.5 %copy-start.6 = (f32[1024,640]{1,0:T(8,128)S(1)}, f32[1024,640]{1,0:T(8,128)}, u32[]{:S(2)}) copy-start(f32[1024,640]{1,0:T(8,128)} %convert_element_type.144) | copy-start | bytes 7864324
  239.7 23.0 %all-to-all-start.5 = ((bf16[4,256,640]{2,1,0:T(8,128)(2,1)}), bf16[4,256,640]{2,1,0:T(8,128)(2,1)}, u32[]{:S(2)}, u32[]{:S(2)}) async-start(bf16[4,256,640]{2,1,0:T(8,128)(2,1)} %bitcast.207), calls=%async_computation.5 | async-start | bytes 2621440 | tf_op jit(solution)/shard_map/all_to_all | solution.py:21
  244.3 751.5 %all-reduce.18.cloned.1.call-start = ((), (), s32[]{:S(2)}) async-start(), calls=%async_computation.8 | async-start | bytes 2621440 | tf_op jit(solution)/shard_map/psum | solution.py:309
  244.3 29.2 %copy-start.8 = (f32[256,640]{1,0:T(8,128)S(1)}, f32[256,640]{1,0:T(8,128)}, u32[]{:S(2)}) copy-start(f32[256,640]{1,0:T(8,128)} %copy-done.7) | copy-start | bytes 1966084
  276.0 6.2 copy-start.62
  276.0 6.2 copy-start.63
  276.0 6.2 copy-start.64
  276.0 212.4 %all-to-all-start.6 = ((bf16[4,256,640]{2,1,0:T(8,128)(2,1)}), bf16[4,256,640]{2,1,0:T(8,128)(2,1)S(1)}, u32[]{:S(2)}, u32[]{:S(2)}) async-start(bf16[4,256,640]{2,1,0:T(8,128)(2,1)} %broadcast_in_dim.101), calls=%async_computation.6 | async-start | bytes 2621440 | tf_op jit(solution)/shard_map/all_to_all | solution.py:33
  638.6 3.8 copy-start.39
  638.6 5.0 copy-start.38
  642.4 2.5 copy-start.37
  995.8 1.5 copy-start.36
  995.8 2.4 copy-start.35
  995.8 3.2 copy-start.1
  (34 other events, 36.7 us)
Sparse Core Ops, SparseCore 0:
  109.3 35.6 all-gather.1
  226.5 46.9 all-reduce.19
  276.9 361.6 all-reduce.21
  641.0 354.7 all-reduce.17
